TPU v7x, 512 devices: a whole 4x8x8 slice. The times are simulated.
512 devices in a mesh: vis: 64 (over y, z), chan: 8 (over x, core).
Axes of the slice: x: 4, y: 8, z: 8, core: 2. Of those that a mesh axis runs over, the one named last changes fastest.
Arguments:
- model: float32 [2, 256, 1024], P(None, 'vis', 'chan'), may hold values from -6 to 6
- kernels: float32 [2, 32, 8], replicated, may hold values from -1.5 to 1.5
- vis_data: float32 [2, 8, 524288], P(None, 'chan', 'vis'), may hold values from -6 to 6
- vis_weight: float32 [8, 524288], P('chan', 'vis'), may hold values from 0.2 to 2
- tile_list: int32 [8, 64, 16], P('chan', 'vis'), may hold values from 0 to 255, as said below
- vis_slot: int32 [8, 524288], P('chan', 'vis'), may hold values from 0 to 15
- vis_wplane: int32 [8, 524288], P('chan', 'vis'), may hold values from 0 to 31
- vis_offset: int32 [2, 8, 524288], P(None, 'chan', 'vis'), may hold values from 0 to 24
Outputs:
- model_step: float32 [2, 256, 1024], P(None, 'vis', 'chan')
- residual: float32 [2, 8, 524288], P(None, 'chan', 'vis')
Inputs may be any that keep to these rules, and one draw needn't show every extreme that they name: `tile_list`: the 16 tiles of one block's list are different and have different owners t // 4.
All inputs are finite; a program needn't handle non-finite values.
Results may differ from a plain program's by a relative error of at most 0.0003.
Values sent between devices are 32-bit elements; how exact they have to be, the bound alone decides.
No kernel may reach another device: no remote copies, remote signals or barrier semaphores. Data moves between devices by JAX's collectives and lax.ppermute only.
A program may use at most 64 MiB of HBM per device.

v0:
```python
import math
import jax
import jax.numpy as jnp
from jax import lax
from jax.sharding import PartitionSpec as P

TILE_SIDE = 32
HIGH = lax.Precision.HIGHEST


def dft_tables(side):
    index = jnp.arange(side, dtype=jnp.int32)
    angle = 2.0 * math.pi / side * (index[:, None] * index[None, :] % side).astype(jnp.float32)
    scale = 1.0 / math.sqrt(side)
    return (jnp.cos(angle) * scale, -jnp.sin(angle) * scale)


def forward(images, cosine, sine):

    def triple(left, right):
        return jnp.einsum("pa,tab,bq->tqp", left, images, right, precision=HIGH)

    return (
        triple(cosine, cosine) - triple(sine, sine),
        triple(cosine, sine) + triple(sine, cosine),
    )


def adjoint(part_re, part_im, cosine, sine):

    def triple(left, middle, right):
        return jnp.einsum("ap,tqp,qb->tab", left, middle, right, precision=HIGH)

    return (
        triple(cosine, part_re, cosine)
        - triple(sine, part_re, sine)
        + triple(sine, part_im, cosine)
        + triple(cosine, part_im, sine)
    )


def place(offset, taps, side):
    rows = jnp.arange(side, dtype=jnp.int32)[:, None]
    shift = rows - offset[None, :]
    total = jnp.zeros((side, offset.shape[0]), jnp.float32)
    for tap in range(taps.shape[0]):
        total = total + jnp.where(shift == tap, taps[tap][None, :], jnp.float32(0.0))
    return total


def crossed(left, right):
    return lax.dot_general(left, right, (((1,), (1,)), ((), ())), precision=HIGH)


def visibility_pass(
    grid_re, grid_im, slot, wplane, off_u, off_v, data_re, data_im, weight, kernels
):
    slots, side = (grid_re.shape[0], grid_re.shape[1])
    planes = kernels.shape[1]
    picker = (jnp.arange(planes, dtype=jnp.int32)[:, None] == wplane[None, :]).astype(jnp.float32)
    taps_re = jnp.dot(kernels[0].T, picker, precision=HIGH)
    taps_im = jnp.dot(kernels[1].T, picker, precision=HIGH)
    a_re = place(off_u, taps_re, side)
    a_im = place(off_u, taps_im, side)
    b_re = place(off_v, taps_re, side)
    b_im = place(off_v, taps_im, side)
    flat_re = grid_re.reshape(slots * side, side)
    flat_im = grid_im.reshape(slots * side, side)
    y_re = jnp.dot(flat_re, a_re, precision=HIGH) - jnp.dot(flat_im, a_im, precision=HIGH)
    y_im = jnp.dot(flat_re, a_im, precision=HIGH) + jnp.dot(flat_im, a_re, precision=HIGH)
    y_re = y_re.reshape(slots, side, -1)
    y_im = y_im.reshape(slots, side, -1)
    owner = (jnp.arange(slots, dtype=jnp.int32)[:, None] == slot[None, :]).astype(jnp.float32)
    pred_re = jnp.sum(owner * jnp.sum(y_re * b_re[None] - y_im * b_im[None], axis=1), axis=0)
    pred_im = jnp.sum(owner * jnp.sum(y_re * b_im[None] + y_im * b_re[None], axis=1), axis=0)
    res_re = weight * (data_re - pred_re)
    res_im = weight * (data_im - pred_im)
    z_re = (owner[:, None, :] * (res_re * b_re + res_im * b_im)[None]).reshape(slots * side, -1)
    z_im = (owner[:, None, :] * (res_im * b_re - res_re * b_im)[None]).reshape(slots * side, -1)
    part_re = crossed(z_re, a_re) + crossed(z_im, a_im)
    part_im = crossed(z_im, a_re) - crossed(z_re, a_im)
    return (res_re, res_im, part_re.reshape(slots, side, side), part_im.reshape(slots, side, side))


def shards(model, kernels, vis_data, vis_weight, tile_list, vis_slot, vis_wplane, vis_offset):
    side = TILE_SIDE
    cells = side * side
    channels = lax.axis_size("chan")
    chan_here = lax.axis_index("chan")
    offsets_all = (jnp.arange(channels, dtype=jnp.float32) - 0.5 * (channels - 1)) / channels
    frequency = jnp.sum(
        jnp.where(jnp.arange(channels, dtype=jnp.int32) == chan_here, offsets_all, jnp.float32(0.0))
    )
    cosine, sine = dft_tables(side)
    listed = tile_list[0, 0]
    slots = listed.shape[0]
    tile_dev = model.shape[1]
    piece_cells = model.shape[2]
    whole = lax.all_gather(model, "chan", axis=2, tiled=True)

    def matches(length):
        return (listed[:, None] == jnp.arange(length, dtype=jnp.int32)[None, :]).astype(jnp.float32)

    image = (whole[0] + frequency * whole[1]).reshape(tile_dev, side, side)
    own_re, own_im = forward(image, cosine, sine)
    packed = jnp.concatenate(
        [own_re.reshape(tile_dev, cells), own_im.reshape(tile_dev, cells)], axis=1
    )
    piece = lax.all_gather(packed, "vis", axis=0, tiled=True)
    chosen = jnp.dot(matches(piece.shape[0]), piece, precision=HIGH)
    grid_re = chosen[:, :cells].reshape(slots, side, side)
    grid_im = chosen[:, cells:].reshape(slots, side, side)
    count = vis_data.shape[2]
    block = min(512, count)
    blocks = count // block

    def rows_of(values):
        return values.reshape(blocks, block)

    sequence = (
        rows_of(vis_slot[0]),
        rows_of(vis_wplane[0]),
        rows_of(vis_offset[0, 0]),
        rows_of(vis_offset[1, 0]),
        rows_of(vis_data[0, 0]),
        rows_of(vis_data[1, 0]),
        rows_of(vis_weight[0]),
    )

    def one_block(carry, inputs):
        slot, wplane, off_u, off_v, data_re, data_im, weight = inputs
        res_re, res_im, part_re, part_im = visibility_pass(
            grid_re, grid_im, slot, wplane, off_u, off_v, data_re, data_im, weight, kernels
        )
        return ((carry[0] + part_re, carry[1] + part_im), (res_re, res_im))

    empty = jnp.zeros((slots, side, side), jnp.float32)
    (acc_re, acc_im), (out_re, out_im) = lax.scan(one_block, (empty, empty), sequence)
    residual = jnp.stack([out_re.reshape(count), out_im.reshape(count)])[:, None, :]
    partial_tiles = jnp.concatenate(
        [acc_re.reshape(slots, cells), acc_im.reshape(slots, cells)], axis=1
    )
    owned = lax.psum_scatter(
        jnp.dot(matches(lax.axis_size("vis") * tile_dev).T, partial_tiles, precision=HIGH),
        "vis",
        scatter_dimension=0,
        tiled=True,
    )
    dirty = adjoint(
        owned[:, :cells].reshape(tile_dev, side, side),
        owned[:, cells:].reshape(tile_dev, side, side),
        cosine,
        sine,
    ).reshape(tile_dev, cells)
    every = lax.all_gather(dirty[None], "chan", axis=0, tiled=True)
    mine = lax.dynamic_slice_in_dim(every, chan_here * piece_cells, piece_cells, 2)
    gradient = jnp.stack(
        [jnp.sum(mine, axis=0), jnp.sum(offsets_all[:, None, None] * mine, axis=0)]
    )
    curvature = jnp.stack([jnp.float32(channels), jnp.sum(offsets_all * offsets_all)])
    model_step = gradient / curvature[:, None, None]
    return (model_step, residual)


def solution(mesh):
    placed = (
        P(None, "vis", "chan"),
        P(),
        P(None, "chan", "vis"),
        P("chan", "vis"),
        P("chan", "vis", None),
        P("chan", "vis"),
        P("chan", "vis"),
        P(None, "chan", "vis"),
    )
    return jax.shard_map(
        shards,
        mesh=mesh,
        in_specs=placed,
        out_specs=(P(None, "vis", "chan"), P(None, "chan", "vis")),
        check_vma=False,
    )
```

profile of v0, /device:TPU:1, one launch (start us, length us, event | category | flops | bytes accessed | tf_op | source)
XLA Modules:
  0.0 474.5 jit_solution(9715506819741355807)
XLA Ops:
  7.9 18.1 %all_gather.9 = f32[2,4,1024]{2,1,0:T(4,128)S(1)} all-gather(f32[2,4,128]{2,1,0:T(4,128)} %param.10), channel_id=1, replica_groups=mesh['vis'=64,'chan'=8] {'chan'}, dimensions={2}, use_global_device_ids=true | all-gather | bytes 36864 | tf_op jit(solution)/shard_map/all_gather | solution.py:99
  34.6 73.3 %all-gather.3.cloned.1.call-done = f32[64,4,2048]{2,1,0:T(4,128)} async-done(((f32[1,4,2048]{2,1,0:T(4,128)}), f32[64,4,2048]{2,1,0:T(4,128)}) %all-gather.3.cloned.1.call-update) | async-done | bytes 2097168 | tf_op jit(solution)/shard_map/all_gather | solution.py:109
  107.9 2.0 reshape.1041
  110.7 171.5 %while.17 = (s32[]{:T(128)}, f32[16,32,32]{1,0,2:T(8,128)S(1)}, f32[16,32,32]{1,0,2:T(8,128)S(1)}, f32[16,512]{1,0:T(8,128)S(1)}, f32[16,512]{1,0:T(8,128)S(1)},...) while((s32[]{:T(128)}, f32[16,32,32]{1,0,2:T(8,128)S(1)}, ...), condition=%wide.region_6.7_spmd.clone, body=%wide.region_1.6_spmd.clone.sunk | while | flops 816292864 | bytes 15255747 | solution.py:138
  114.6 1.4 subtract_reduce_fusion.2
  117.6 1.1 convolution_add_fusion.6
  119.9 1.1 convolution_subtract_fusion.7
  125.3 1.4 subtract_reduce_fusion.2
  128.3 1.1 convolution_add_fusion.6
  130.6 1.1 convolution_subtract_fusion.7
  136.0 1.4 subtract_reduce_fusion.2
  139.0 1.1 convolution_add_fusion.6
  141.4 1.1 convolution_subtract_fusion.7
  146.8 1.4 subtract_reduce_fusion.2
  149.7 1.1 convolution_add_fusion.6
  152.1 1.1 convolution_subtract_fusion.7
  157.5 1.4 subtract_reduce_fusion.2
  160.5 1.1 convolution_add_fusion.6
  162.8 1.1 convolution_subtract_fusion.7
  168.2 1.4 subtract_reduce_fusion.2
  171.2 1.1 convolution_add_fusion.6
  173.5 1.1 convolution_subtract_fusion.7
  178.9 1.4 subtract_reduce_fusion.2
  181.9 1.1 convolution_add_fusion.6
  184.2 1.1 convolution_subtract_fusion.7
  189.6 1.4 subtract_reduce_fusion.2
  192.6 1.1 convolution_add_fusion.6
  195.0 1.1 convolution_subtract_fusion.7
  200.4 1.4 subtract_reduce_fusion.2
  205.7 1.1 convolution_subtract_fusion.7
  211.1 1.4 subtract_reduce_fusion.2
  216.4 1.1 convolution_subtract_fusion.7
  221.8 1.4 subtract_reduce_fusion.2
  227.1 1.1 convolution_subtract_fusion.7
  232.5 1.4 subtract_reduce_fusion.2
  237.8 1.1 convolution_subtract_fusion.7
  243.2 1.4 subtract_reduce_fusion.2
  248.6 1.1 convolution_subtract_fusion.7
  254.0 1.4 subtract_reduce_fusion.2
  259.3 1.1 convolution_subtract_fusion.7
  264.7 1.4 subtract_reduce_fusion.2
  270.0 1.1 convolution_subtract_fusion.7
  275.4 1.4 subtract_reduce_fusion.2
  280.7 1.1 convolution_subtract_fusion.7
  282.9 2.4 fusion.101
  285.3 1.3 dynamic-slice
  289.6 156.2 %all-reduce.3.cloned.1.call-done = f32[256,2048]{1,0:T(8,128)} async-done(((f32[256,2048]{1,0:T(8,128)}), f32[256,2048]{1,0:T(8,128)}) %all-reduce.3.cloned.1.call-update) | async-done | bytes 2097168
  449.8 17.2 %all_gather.11 = f32[8,4,1024]{2,1,0:T(4,128)S(1)} all-gather(f32[1,4,1024]{2,1,0:T(4,128)S(1)} %broadcast_in_dim_reshape.3), channel_id=1, replica_groups=mesh['vis'=64,'chan'=8] {'chan'}, dimensions={0}, use_global_device_ids=true | all-gather | bytes 147456 | tf_op jit(solution)/shard_map/all_gather | solution.py:155
  (497 shorter events, 136.5 us)
Async XLA Ops:
  7.2 24.8 %copy-start.1 = (s32[1,8192]{1,0:T(1,128)S(1)}, s32[1,8192]{1,0:T(1,128)}, u32[]{:S(2)}) copy-start(s32[1,8192]{1,0:T(1,128)} %param.15) | copy-start | bytes 98308
  7.2 25.5 %copy-start.2 = (s32[1,8192]{1,0:T(1,128)S(1)}, s32[1,8192]{1,0:T(1,128)}, u32[]{:S(2)}) copy-start(s32[1,8192]{1,0:T(1,128)} %param.16) | copy-start | bytes 98308
  7.2 26.7 %copy-start.3 = (f32[1,8192]{1,0:T(1,128)S(1)}, f32[1,8192]{1,0:T(1,128)}, u32[]{:S(2)}) copy-start(f32[1,8192]{1,0:T(1,128)} %param.13) | copy-start | bytes 98308
  7.2 100.7 %all-gather.3.cloned.1.call-start = ((), (), s32[]{:S(2)}) async-start(), calls=%async_computation | async-start | bytes 2129920 | tf_op jit(solution)/shard_map/all_gather | solution.py:109
  29.4 416.4 %all-reduce.3.cloned.1.call-start = ((), (), s32[]{:S(2)}) async-start(), calls=%async_computation.1 | async-start | bytes 4194304
  34.6 75.3 %copy-start.4 = (s32[1,1,16]{2,1,0:T(1,128)S(1)}, s32[1,1,16]{2,1,0:T(1,128)}, u32[]{:S(2)}) copy-start(s32[1,1,16]{2,1,0:T(1,128)} %param.14) | copy-start | bytes 196
  109.9 0.9 copy-start
Sparse Core Ops, SparseCore 0:
  29.5 78.3 all-gather.2
  285.4 160.3 all-reduce.2
where the time goes:
time: 475 us
  waiting for transfers between devices  230 us (48%)
  matrix products  155 us (33%)
  blocking collectives  35.3 us (7%)
  local copies, waits for them, and re-layouts  19.6 us (4%)
  other arithmetic  16.9 us (4%)
  between operations  15 us (3%)
    unnamed x3, waiting for transfers between devices  156 us
    all_gather x1, waiting for transfers between devices, shards(): piece = lax.all_gather(packed, 'vis', axis=0, tiled=True)  73.3 us
    dot_general x64, matrix products, crossed(): lax.dot_general(left, right, (((1,), (1,)), ((), ())), precision=HIGH)  70.7 us
    dot_general x16, matrix products, visibility_pass(): jnp.dot(flat_im, a_re, precision=HIGH)  22.7 us
    all_gather x1, blocking collectives, shards(): whole = lax.all_gather(model, 'chan', axis=2, tiled=True)  18.1 us
    all_gather x1, blocking collectives, shards(): every = lax.all_gather(dirty[None], 'chan', axis=0, tiled=True)  17.2 us
    dot_general x16, matrix products, visibility_pass(): jnp.dot(flat_im, a_im, precision=HIGH)  16.9 us
    dot_general x16, matrix products, visibility_pass(): jnp.dot(flat_re, a_re, precision=HIGH)  16.4 us
  transfers between devices with their start and end apart: 2, of which 2 were waited for; matrix products, arithmetic and copies ran while one was open for 2% of the time, Pallas kernels for 0%

commit v1 on v0

--- a/solution.py
+++ b/solution.py
@@ -96,7 +96,21 @@
     slots = listed.shape[0]
     tile_dev = model.shape[1]
     piece_cells = model.shape[2]
-    whole = lax.all_gather(model, "chan", axis=2, tiled=True)
+    ways, here, step = (lax.axis_size("chan"), lax.axis_index("chan"), model.shape[2])
+    dims = [n * ways if d == 2 else n for d, n in enumerate(model.shape)]
+    full = lax.dynamic_update_slice_in_dim(jnp.zeros(dims, model.dtype), model, here * step, axis=2)
+    going_up = going_down = model
+    for far in range(1, ways // 2 + 1):
+        going_up = lax.ppermute(going_up, "chan", [(d, (d + 1) % ways) for d in range(ways)])
+        full = lax.dynamic_update_slice_in_dim(full, going_up, (here - far) % ways * step, axis=2)
+        if 2 * far < ways:
+            going_down = lax.ppermute(
+                going_down, "chan", [(d, (d - 1) % ways) for d in range(ways)]
+            )
+            full = lax.dynamic_update_slice_in_dim(
+                full, going_down, (here + far) % ways * step, axis=2
+            )
+    whole = full
 
     def matches(length):
         return (listed[:, None] == jnp.arange(length, dtype=jnp.int32)[None, :]).astype(jnp.float32)

time: 475 us -> 478 us (level)
  blocking collectives: 35.3 us -> 17.2 us
  starting transfers between devices: 0.08 us -> 13.6 us
  waiting for transfers between devices: 230 us -> 237 us
    all_gather x1 -> x0, blocking collectives: 18.1 us -> none  [shards(): whole = lax.all_gather(model, 'chan', axis=2, tiled=True)]
    ppermute x0 -> x7, starting transfers between devices: none -> 13.5 us  [the longest x3 10.9 us: shards(): lax.ppermute(going_down, 'chan', [(d, (d - 1) % ways) for d in range(ways)])]
    ppermute x0 -> x7, waiting for transfers between devices: none -> 5.63 us  [the longest x4 5.22 us: shards(): lax.ppermute(going_up, 'chan', [(d, (d + 1) % ways) for d in range(ways)])]
  transfers between devices with their start and end apart: 2 -> 9, of which waited for: 2 -> 7; matrix products, arithmetic and copies ran while one was open for 2% -> 2% of each run, Pallas kernels for 0% -> 0%
where the time goes in v1:
time: 478 us
  waiting for transfers between devices  237 us (50%)
  matrix products  155 us (32%)
  local copies, waits for them, and re-layouts  19.6 us (4%)
  blocking collectives  17.2 us (4%)
  other arithmetic  16.9 us (4%)
  between operations  15 us (3%)
  starting transfers between devices  13.6 us (3%)
    unnamed x3, waiting for transfers between devices  156 us
    all_gather x1, waiting for transfers between devices, shards(): piece = lax.all_gather(packed, 'vis', axis=0, tiled=True)  75.3 us
    dot_general x64, matrix products, crossed(): lax.dot_general(left, right, (((1,), (1,)), ((), ())), precision=HIGH)  70.7 us
    dot_general x16, matrix products, visibility_pass(): jnp.dot(flat_im, a_re, precision=HIGH)  22.7 us
    all_gather x1, blocking collectives, shards(): every = lax.all_gather(dirty[None], 'chan', axis=0, tiled=True)  17.2 us
    dot_general x16, matrix products, visibility_pass(): jnp.dot(flat_im, a_im, precision=HIGH)  16.9 us
    dot_general x16, matrix products, visibility_pass(): jnp.dot(flat_re, a_re, precision=HIGH)  16.4 us
    dot_general x16, matrix products, visibility_pass(): jnp.dot(flat_re, a_im, precision=HIGH)  16.3 us
  transfers between devices with their start and end apart: 9, of which 7 were waited for; matrix products, arithmetic and copies ran while one was open for 2% of the time, Pallas kernels for 0%

profile of v1, /device:TPU:1, one launch (start us, length us, event | category | flops | bytes accessed | tf_op | source)
XLA Modules:
  0.0 477.5 jit_solution(8353356667395095648)
XLA Ops:
  7.3 2.6 collective-permute-start
  9.9 4.3 collective-permute-start.1
  15.5 3.2 collective-permute-start.3
  19.5 3.4 collective-permute-start.5
  23.7 4.0 collective-permute-done.6
  35.6 75.3 %all-gather.3.cloned.1.call-done = f32[64,4,2048]{2,1,0:T(4,128)} async-done(((f32[1,4,2048]{2,1,0:T(4,128)}), f32[64,4,2048]{2,1,0:T(4,128)}) %all-gather.3.cloned.1.call-update) | async-done | bytes 2097168 | tf_op jit(solution)/shard_map/all_gather | solution.py:123
  110.9 2.0 reshape.1041
  113.7 171.5 %while.17 = (s32[]{:T(128)}, f32[16,32,32]{1,0,2:T(8,128)S(1)}, f32[16,32,32]{1,0,2:T(8,128)S(1)}, f32[16,512]{1,0:T(8,128)S(1)}, f32[16,512]{1,0:T(8,128)S(1)},...) while((s32[]{:T(128)}, f32[16,32,32]{1,0,2:T(8,128)S(1)}, ...), condition=%wide.region_6.7_spmd.clone, body=%wide.region_1.6_spmd.clone.sunk | while | flops 816292864 | bytes 15255747 | solution.py:152
  117.6 1.4 subtract_reduce_fusion.2
  120.6 1.1 convolution_add_fusion.6
  122.9 1.1 convolution_subtract_fusion.7
  128.3 1.4 subtract_reduce_fusion.2
  131.3 1.1 convolution_add_fusion.6
  133.6 1.1 convolution_subtract_fusion.7
  139.0 1.4 subtract_reduce_fusion.2
  142.0 1.1 convolution_add_fusion.6
  144.3 1.1 convolution_subtract_fusion.7
  149.7 1.4 subtract_reduce_fusion.2
  152.7 1.1 convolution_add_fusion.6
  155.1 1.1 convolution_subtract_fusion.7
  160.5 1.4 subtract_reduce_fusion.2
  165.8 1.1 convolution_subtract_fusion.7
  171.2 1.4 subtract_reduce_fusion.2
  176.5 1.1 convolution_subtract_fusion.7
  181.9 1.4 subtract_reduce_fusion.2
  187.2 1.1 convolution_subtract_fusion.7
  192.6 1.4 subtract_reduce_fusion.2
  197.9 1.1 convolution_subtract_fusion.7
  203.3 1.4 subtract_reduce_fusion.2
  208.7 1.1 convolution_subtract_fusion.7
  214.1 1.4 subtract_reduce_fusion.2
  219.4 1.1 convolution_subtract_fusion.7
  224.8 1.4 subtract_reduce_fusion.2
  230.1 1.1 convolution_subtract_fusion.7
  235.5 1.4 subtract_reduce_fusion.2
  240.8 1.1 convolution_subtract_fusion.7
  246.2 1.4 subtract_reduce_fusion.2
  251.5 1.1 convolution_subtract_fusion.7
  256.9 1.4 subtract_reduce_fusion.2
  262.3 1.1 convolution_subtract_fusion.7
  267.7 1.4 subtract_reduce_fusion.2
  273.0 1.1 convolution_subtract_fusion.7
  278.4 1.4 subtract_reduce_fusion.2
  283.7 1.1 convolution_subtract_fusion.7
  285.9 2.4 fusion.101
  288.3 1.3 dynamic-slice
  292.6 156.2 %all-reduce.3.cloned.1.call-done = f32[256,2048]{1,0:T(8,128)} async-done(((f32[256,2048]{1,0:T(8,128)}), f32[256,2048]{1,0:T(8,128)}) %all-reduce.3.cloned.1.call-update) | async-done | bytes 2097168
  452.8 17.2 %all_gather.7 = f32[8,4,1024]{2,1,0:T(4,128)S(1)} all-gather(f32[1,4,1024]{2,1,0:T(4,128)S(1)} %broadcast_in_dim_reshape.3), channel_id=1, replica_groups=mesh['vis'=64,'chan'=8] {'chan'}, dimensions={0}, use_global_device_ids=true | all-gather | bytes 147456 | tf_op jit(solution)/shard_map/all_gather | solution.py:169
  (521 shorter events, 142.5 us)
Async XLA Ops:
  7.2 25.1 %copy-start.1 = (s32[2,1,8192]{2,1,0:T(1,128)S(1)}, s32[2,1,8192]{2,1,0:T(1,128)}, u32[]{:S(2)}) copy-start(s32[2,1,8192]{2,1,0:T(1,128)} %param.17) | copy-start | bytes 196612
  7.2 25.8 %copy-start.2 = (s32[1,8192]{1,0:T(1,128)S(1)}, s32[1,8192]{1,0:T(1,128)}, u32[]{:S(2)}) copy-start(s32[1,8192]{1,0:T(1,128)} %param.15) | copy-start | bytes 98308
  7.2 26.5 %copy-start.3 = (s32[1,8192]{1,0:T(1,128)S(1)}, s32[1,8192]{1,0:T(1,128)}, u32[]{:S(2)}) copy-start(s32[1,8192]{1,0:T(1,128)} %param.16) | copy-start | bytes 98308
  7.2 27.7 %copy-start.4 = (f32[1,8192]{1,0:T(1,128)S(1)}, f32[1,8192]{1,0:T(1,128)}, u32[]{:S(2)}) copy-start(f32[1,8192]{1,0:T(1,128)} %param.13) | copy-start | bytes 98308
  7.2 103.7 %all-gather.3.cloned.1.call-start = ((), (), s32[]{:S(2)}) async-start(), calls=%async_computation | async-start | bytes 2129920 | tf_op jit(solution)/shard_map/all_gather | solution.py:123
  7.3 8.2 %collective-permute-start = (f32[2,4,128]{2,1,0:T(4,128)}, f32[2,4,128]{2,1,0:T(4,128)S(1)}, u32[]{:S(2)}, u32[]{:S(2)}) collective-permute-start(f32[2,4,128]{2,1,0:T(4,128)} %param.10), channel_id=1, source_target_pairs={{0,1},{1,2},{2,3},{3,4},{4,5},{5,6},{6,7},{7,0},{8,9},{9,10},{10,1... | collective-permute-start | bytes 12296 | tf_op jit(solution)/shard_map/ppermute | solution.py:104
  9.9 5.6 %collective-permute-start.1 = (f32[2,4,128]{2,1,0:T(4,128)}, f32[2,4,128]{2,1,0:T(4,128)S(1)}, u32[]{:S(2)}, u32[]{:S(2)}) collective-permute-start(f32[2,4,128]{2,1,0:T(4,128)} %param.10), channel_id=1, source_target_pairs={{0,7},{1,0},{2,1},{3,2},{4,3},{5,4},{6,5},{7,6},{8,15},{9,8},{10,9... | collective-permute-start | bytes 12296 | tf_op jit(solution)/shard_map/ppermute | solution.py:107
  15.5 3.8 collective-permute-start.2
  15.5 4.0 collective-permute-start.3
  19.3 4.2 collective-permute-start.4
  19.5 4.2 collective-permute-start.5
  23.5 4.2 collective-permute-start.6
  31.2 417.6 %all-reduce.3.cloned.1.call-start = ((), (), s32[]{:S(2)}) async-start(), calls=%async_computation.1 | async-start | bytes 4194304
  35.6 77.3 %copy-start.5 = (s32[1,1,16]{2,1,0:T(1,128)S(1)}, s32[1,1,16]{2,1,0:T(1,128)}, u32[]{:S(2)}) copy-start(s32[1,1,16]{2,1,0:T(1,128)} %param.14) | copy-start | bytes 196
  112.9 0.9 copy-start
Sparse Core Ops, SparseCore 0:
  31.3 79.5 all-gather.2
  288.4 160.3 all-reduce.2
